TPU v7x, 512 devices: a whole 4x8x8 slice. The times are simulated.
512 devices in a mesh: frame: 32 (over y, z_lo, core), tensor: 16 (over x, z_hi).
Axes of the slice: x: 4, y: 8, z: 8 (z_hi: 4, z_lo: 2; z = z_hi * 2 + z_lo), core: 2. Of those that a mesh axis runs over, the one named last changes fastest.
Arguments:
- frames_in: bfloat16 [32, 256, 2048], P('frame', None, 'tensor'), may hold values from -6 to 6
- spatial_gain: float32 [2048], replicated, may hold values from 0.25 to 1.75
- spatial_qkv: bfloat16 [2048, 3, 2048], P('frame', None, 'tensor'), may hold values from -0.125 to 0.125
- spatial_out: bfloat16 [2048, 2048], P('frame', 'tensor'), may hold values from -0.125 to 0.125
- spatial_up: bfloat16 [2048, 4096], P('frame', 'tensor'), may hold values from -0.125 to 0.125
- spatial_down: bfloat16 [2048, 4096], P('frame', 'tensor'), may hold values from -0.09375 to 0.09375
- temporal_gain: float32 [2048], replicated, may hold values from 0.25 to 1.75
- temporal_qkv: bfloat16 [2048, 3, 2048], P('frame', None, 'tensor'), may hold values from -0.125 to 0.125
- temporal_out: bfloat16 [2048, 2048], P('frame', 'tensor'), may hold values from -0.125 to 0.125
- temporal_up: bfloat16 [2048, 4096], P('frame', 'tensor'), may hold values from -0.125 to 0.125
- temporal_down: bfloat16 [2048, 4096], P('frame', 'tensor'), may hold values from -0.09375 to 0.09375
Outputs:
- encoded: bfloat16 [32, 256, 2048], P(None, 'frame', 'tensor')
All inputs are finite; a program needn't handle non-finite values.
Results may differ from a plain program's by a relative error of at most 0.022.
Values may be sent and summed in bfloat16 or wider, within the bound.
A program may use at most 64 MiB of HBM per device.

v0:
```python
import jax
import jax.numpy as jnp
from jax import lax
from jax.sharding import PartitionSpec as P

HEAD_DIM = 128


EPS = 1e-06


def norm_rows(values, gain):
    centered = values - jnp.mean(values, axis=-1, keepdims=True)
    spread = jnp.mean(centered * centered, axis=-1, keepdims=True)
    return centered * lax.rsqrt(spread + EPS) * gain


def attend(qkv, time_major):
    query = norm_rows(qkv[:, :, 0], 1.0).astype(jnp.bfloat16)
    keys = norm_rows(qkv[:, :, 1], 1.0).astype(jnp.bfloat16)
    values = qkv[:, :, 2].astype(jnp.bfloat16)
    if time_major:
        first, second = ("qbhd,kbhd->bhqk", "bhqk,kbhd->qbhd")
    else:
        first, second = ("bqhd,bkhd->bhqk", "bhqk,bkhd->bqhd")
    scores = jnp.einsum(first, query, keys, preferred_element_type=jnp.float32) * qkv.shape[-1] ** (
        -0.5
    )
    expo = jnp.exp(scores)
    weights = (expo / jnp.sum(expo, axis=-1, keepdims=True)).astype(jnp.bfloat16)
    return jnp.einsum(second, weights, values, preferred_element_type=jnp.float32).astype(
        jnp.bfloat16
    )


def branch_terms(inputs, gain, qkv_weight, out_weight, up_weight, down_weight, time_major):
    first, second, width = inputs.shape
    flat = norm_rows(inputs.astype(jnp.float32), gain).astype(jnp.bfloat16).reshape(-1, width)
    rows = flat.shape[0]
    cols = qkv_weight.shape[2]

    def add_one(piece):
        count = piece.shape[0]
        return jnp.dot(flat, piece.reshape(count, -1), preferred_element_type=jnp.float32)

    qkv = add_one(lax.all_gather(qkv_weight, "frame", axis=0, tiled=True))
    up_total = add_one(lax.all_gather(up_weight, "frame", axis=0, tiled=True))
    heads = cols // HEAD_DIM
    mixed = attend(qkv.reshape(first, second, 3, heads, HEAD_DIM), time_major).reshape(rows, cols)
    hidden = jax.nn.gelu(up_total, approximate=True).astype(jnp.bfloat16)
    contract = (((1,), (1,)), ((), ()))
    pieces = lax.all_gather((out_weight, down_weight), "frame", axis=0, tiled=True)
    term = lax.dot_general(mixed, pieces[0], contract, preferred_element_type=jnp.float32)
    return term + lax.dot_general(hidden, pieces[1], contract, preferred_element_type=jnp.float32)


def body(
    frames_in,
    spatial_gain,
    spatial_qkv,
    spatial_out,
    spatial_up,
    spatial_down,
    temporal_gain,
    temporal_qkv,
    temporal_out,
    temporal_up,
    temporal_down,
):
    frame_count, patch_count, feature_cols = frames_in.shape
    whole = lax.all_gather(frames_in, "tensor", axis=2, tiled=True)
    partial_value = branch_terms(
        whole, spatial_gain, spatial_qkv, spatial_out, spatial_up, spatial_down, False
    )
    summed = lax.psum(partial_value.astype(jnp.bfloat16), "tensor").astype(jnp.float32)
    middle = (whole.astype(jnp.float32) + summed.reshape(whole.shape)).astype(jnp.bfloat16)
    after = lax.all_to_all(middle, "frame", split_axis=1, concat_axis=0, tiled=True)
    offset = lax.axis_index("tensor") * feature_cols
    resid = lax.dynamic_slice_in_dim(after, offset, feature_cols, 2)
    partial_value = branch_terms(
        after, temporal_gain, temporal_qkv, temporal_out, temporal_up, temporal_down, True
    )
    share = lax.psum_scatter(
        partial_value.reshape(after.shape[0], after.shape[1], -1).astype(jnp.bfloat16),
        "tensor",
        scatter_dimension=2,
        tiled=True,
    ).astype(jnp.float32)
    return (resid.astype(jnp.float32) + share).astype(jnp.bfloat16)


def solution(mesh):
    in_specs = (
        P("frame", None, "tensor"),
        P(),
        P("frame", None, "tensor"),
        P("frame", "tensor"),
        P("frame", "tensor"),
        P("frame", "tensor"),
        P(),
        P("frame", None, "tensor"),
        P("frame", "tensor"),
        P("frame", "tensor"),
        P("frame", "tensor"),
    )
    out_specs = P(None, "frame", "tensor")
    return jax.shard_map(body, mesh=mesh, in_specs=in_specs, out_specs=out_specs, check_vma=False)
```

profile of v0, /device:TPU:1, one launch (start us, length us, event | category | flops | bytes accessed | tf_op | source)
XLA Modules:
  0.0 818.5 jit_solution(1840609599868127079)
XLA Ops:
  9.4 41.5 %all_gather.29 = bf16[2048,128]{1,0:T(8,128)(2,1)} all-gather(bf16[64,128]{1,0:T(8,128)(2,1)} %param.14), channel_id=1, replica_groups=mesh['frame'=32,'tensor'=16] {'frame'}, dimensions={0}, use_global_device_ids=true | all-gather | bytes 540672 | tf_op jit(solution)/shard_map/all_gather | solution.py:52
  50.8 25.2 %all-gather.8.cloned.1.call-done = bf16[1,256,2048]{2,1,0:T(8,128)(2,1)} async-done(((bf16[1,256,128]{2,1,0:T(8,128)(2,1)}), bf16[1,256,2048]{2,1,0:T(8,128)(2,1)}) %all-gather.8.cloned.1.call-update) | async-done | bytes 1048592 | tf_op jit(solution)/shard_map/all_gather | solution.py:71
  76.1 1.4 convert_reduce_fusion.1
  77.5 1.7 fusion.11
  79.3 63.4 %all-gather.10.cloned.1.call-done = bf16[2048,3,128]{2,0,1:T(8,128)(2,1)} async-done(((bf16[64,3,128]{2,0,1:T(8,128)(2,1)}), bf16[2048,3,128]{2,0,1:T(8,128)(2,1)}) %all-gather.10.cloned.1.call-update) | async-done | bytes 1572880 | tf_op jit(solution)/shard_map/all_gather | solution.py:46
  142.7 1.7 copy.31
  144.4 0.7 fusion.23
  145.3 0.9 fusion.136
  146.2 1.8 fusion.33
  148.0 62.9 %all-gather.12.cloned.1.call-done = bf16[2048,256]{1,0:T(8,128)(2,1)} async-done(((bf16[64,256]{1,0:T(8,128)(2,1)}), bf16[2048,256]{1,0:T(8,128)(2,1)}) %all-gather.12.cloned.1.call-update) | async-done | bytes 1048592 | tf_op jit(solution)/shard_map/all_gather | solution.py:47
  210.9 68.1 %all-gather.14.cloned.1.call-done = bf16[2048,256]{1,0:T(8,128)(2,1)} async-done(((bf16[64,256]{1,0:T(8,128)(2,1)}), bf16[2048,256]{1,0:T(8,128)(2,1)}) %all-gather.14.cloned.1.call-update) | async-done | bytes 1048592 | tf_op jit(solution)/shard_map/all_gather | solution.py:52
  279.0 3.9 fusion.7
  284.2 164.2 %all-reduce.2.cloned.1.call-done = bf16[1,256,2048]{2,1,0:T(8,128)(2,1)} async-done(((bf16[1,256,2048]{2,1,0:T(8,128)(2,1)}), bf16[1,256,2048]{2,1,0:T(8,128)(2,1)}) %all-reduce.2.cloned.1.call-update) | async-done | bytes 1048592 | tf_op jit(solution)/shard_map/psum | solution.py:75
  448.4 1.6 fusion.14
  450.0 1.6 copy.61
  452.2 6.8 reduce.20
  459.0 1.9 reshape.425
  460.9 18.1 %all-to-all-start = ((bf16[32,2,8192]{2,1,0:T(2,128)(2,1)}), bf16[32,2,8192]{2,1,0:T(2,128)(2,1)S(1)}, u32[]{:S(2)}, u32[]{:S(2)}) async-start(bf16[32,2,8192]{2,1,0:T(2,128)(2,1)} %reshape.425), calls=%async_computation | async-start | bytes 2097152 | tf_op jit(solution)/shard_map/all_to_all | solution.py:77
  479.8 58.6 %all_gather.33 = bf16[2048,128]{1,0:T(8,128)(2,1)} all-gather(bf16[64,128]{1,0:T(8,128)(2,1)S(1)} %copy-done.2), channel_id=1, replica_groups=mesh['frame'=32,'tensor'=16] {'frame'}, dimensions={0}, use_global_device_ids=true | all-gather | bytes 540672 | tf_op jit(solution)/shard_map/all_gather | solution.py:52
  538.3 2.7 copy.34
  541.0 1.0 reshape.426
  542.1 0.8 convert_reduce_fusion
  543.5 0.8 fusion.26
  545.4 1.5 fusion.106
  546.8 51.4 %all-gather.18.cloned.1.call-done = bf16[2048,256]{1,0:T(8,128)(2,1)} async-done(((bf16[64,256]{1,0:T(8,128)(2,1)}), bf16[2048,256]{1,0:T(8,128)(2,1)}) %all-gather.18.cloned.1.call-update) | async-done | bytes 1048592 | tf_op jit(solution)/shard_map/all_gather | solution.py:47
  598.2 68.5 %all-gather.20.cloned.1.call-done = bf16[2048,256]{1,0:T(8,128)(2,1)} async-done(((bf16[64,256]{1,0:T(8,128)(2,1)}), bf16[2048,256]{1,0:T(8,128)(2,1)}) %all-gather.20.cloned.1.call-update) | async-done | bytes 1048592 | tf_op jit(solution)/shard_map/all_gather | solution.py:52
  666.7 3.9 fusion.6
  670.6 23.1 %copy.42 = bf16[32,8,2048]{1,0,2:T(8,128)(2,1)} copy(bf16[32,8,2048]{2,1,0:T(8,128)(2,1)} %fusion.6) | data formatting | bytes 2097152
  693.7 24.5 %reshape.422 = bf16[2048,256]{1,0:T(8,128)(2,1)} reshape(bf16[2048,32,8]{2,1,0:T(8,128)(2,1)} %bitcast.148) | data formatting | bytes 2097152
  718.2 89.9 %reduce-scatter.4.cloned.1.call-done = bf16[128,256]{1,0:T(8,128)(2,1)} async-done(((bf16[2048,256]{1,0:T(8,128)(2,1)}), bf16[128,256]{1,0:T(8,128)(2,1)}) %reduce-scatter.4.cloned.1.call-update) | async-done | bytes 65552
  808.1 2.1 reshape.423
  810.2 1.1 copy.43
  (54 shorter events, 7.8 us)
Async XLA Ops:
  6.5 69.5 %all-gather.8.cloned.1.call-start = ((), (), s32[]{:S(2)}) async-start(), calls=%async_computation.2 | async-start | bytes 1114112 | tf_op jit(solution)/shard_map/all_gather | solution.py:71
  7.3 135.4 %all-gather.10.cloned.1.call-start = ((), (), s32[]{:S(2)}) async-start(), calls=%async_computation.3 | async-start | bytes 1622016 | tf_op jit(solution)/shard_map/all_gather | solution.py:46
  8.0 202.9 %all-gather.12.cloned.1.call-start = ((), (), s32[]{:S(2)}) async-start(), calls=%async_computation.4 | async-start | bytes 1081344 | tf_op jit(solution)/shard_map/all_gather | solution.py:47
  8.7 270.3 %all-gather.14.cloned.1.call-start = ((), (), s32[]{:S(2)}) async-start(), calls=%async_computation.5 | async-start | bytes 1081344 | tf_op jit(solution)/shard_map/all_gather | solution.py:52
  9.3 439.1 %all-reduce.2.cloned.1.call-start = ((), (), s32[]{:S(2)}) async-start(), calls=%async_computation.6 | async-start | bytes 2097152 | tf_op jit(solution)/shard_map/psum | solution.py:75
  77.5 66.9 %copy-start = (bf16[1,256,2048]{2,1,0:T(8,128)(2,1)S(1)}, bf16[1,256,2048]{2,1,0:T(8,128)(2,1)}, u32[]{:S(2)}) copy-start(bf16[1,256,2048]{2,1,0:T(8,128)(2,1)} %all-gather.8.cloned.1.call-done) | copy-start | bytes 3145732
  77.5 66.9 %copy-start.3 = (f32[2048]{0:T(1024)S(1)}, f32[2048]{0:T(1024)}, u32[]{:S(2)}) copy-start(f32[2048]{0:T(1024)} %param.12) | copy-start | bytes 24580
  79.3 65.9 %copy-start.5 = (f32[256]{0:T(256)}, f32[256]{0:T(256)S(1)}, u32[]{:S(2)}) copy-start(f32[256]{0:T(256)S(1)} %add_rsqrt_fusion.5) | copy-start | bytes 3076
  282.9 255.4 %all-gather.16.cloned.1.call-start = ((), (), s32[]{:S(2)}) async-start(), calls=%async_computation.7 | async-start | bytes 1622016 | tf_op jit(solution)/shard_map/all_gather | solution.py:46
  283.5 314.7 %all-gather.18.cloned.1.call-start = ((), (), s32[]{:S(2)}) async-start(), calls=%async_computation.8 | async-start | bytes 1081344 | tf_op jit(solution)/shard_map/all_gather | solution.py:47
  459.0 20.8 %copy-start.2 = (bf16[64,128]{1,0:T(8,128)(2,1)S(1)}, bf16[64,128]{1,0:T(8,128)(2,1)}, u32[]{:S(2)}) copy-start(bf16[64,128]{1,0:T(8,128)(2,1)} %param.19) | copy-start | bytes 49156
  460.9 80.1 %all-to-all-start = ((bf16[32,2,8192]{2,1,0:T(2,128)(2,1)}), bf16[32,2,8192]{2,1,0:T(2,128)(2,1)S(1)}, u32[]{:S(2)}, u32[]{:S(2)}) async-start(bf16[32,2,8192]{2,1,0:T(2,128)(2,1)} %reshape.425), calls=%async_computation | async-start | bytes 2097152 | tf_op jit(solution)/shard_map/all_to_all | solution.py:77
  479.0 187.7 %all-gather.20.cloned.1.call-start = ((), (), s32[]{:S(2)}) async-start(), calls=%async_computation.9 | async-start | bytes 1081344 | tf_op jit(solution)/shard_map/all_gather | solution.py:52
  479.7 328.4 %reduce-scatter.4.cloned.1.call-start = ((), (), s32[]{:S(2)}) async-start(), calls=%async_computation.10 | async-start | bytes 1114112
  542.1 1.4 copy-start.1
  542.1 1.4 copy-start.4
Sparse Core Ops, SparseCore 0:
  10.3 65.6 all-gather.7
  78.2 64.4 all-gather.9
  144.8 66.0 all-gather.11
  212.9 66.0 all-gather.13
  283.0 165.3 all-reduce.1
  450.7 78.2 all-gather.15
  531.3 66.8 all-gather.17
  600.6 66.0 all-gather.19
  718.4 89.7 reduce-scatter.3
where the time goes:
time: 820 us; the launch traced here: 818 us
  waiting for transfers between devices  598 us (73%)
  blocking collectives  100 us (12%)
  local copies, waits for them, and re-layouts  60.4 us (7%)
  starting transfers between devices  18.6 us (2%)
  other arithmetic  14.2 us (2%)
  matrix products  13.9 us (2%)
  between operations  13.5 us (2%)
    psum x1, waiting for transfers between devices, body(): lax.psum(partial_value.astype(jnp.bfloat16), 'tensor').astype(jnp.float32)  164 us
    all_gather x2, waiting for transfers between devices, branch_terms(): lax.all_gather((out_weight, down_weight), 'frame', axis=0, tiled=True)  137 us
    all_gather x2, waiting for transfers between devices, branch_terms(): up_total = add_one(lax.all_gather(up_weight, 'frame', axis=0, tiled=True))  114 us
    all_gather x2, blocking collectives, branch_terms(): lax.all_gather((out_weight, down_weight), 'frame', axis=0, tiled=True)  100 us
    unnamed x10, waiting for transfers between devices  94.2 us
    all_gather x2, waiting for transfers between devices, branch_terms(): qkv = add_one(lax.all_gather(qkv_weight, 'frame', axis=0, tiled=True))  63.4 us
    unnamed x19, local copies, waits for them, and re-layouts  54.4 us
    all_gather x1, waiting for transfers between devices, body(): whole = lax.all_gather(frames_in, 'tensor', axis=2, tiled=True)  25.2 us
  transfers between devices with their start and end apart: 10, of which 8 were waited for; matrix products, arithmetic and copies ran while one was open for 4% of the time, Pallas kernels for 0%

commit v1 on v0

v1 whole, which is shorter than its diff:
```python
import jax
import jax.numpy as jnp
from jax import lax
from jax.experimental import pallas as pl
from jax.experimental.pallas import tpu as pltpu
from jax.sharding import PartitionSpec as P

MESH = pl.DeviceIdType.MESH
EPS = 1e-06
BF = jnp.bfloat16
F32 = jnp.float32
NT = (((1,), (1,)), ((), ()))


def norm_rows(values):
    centered = values - jnp.mean(values, axis=-1, keepdims=True)
    spread = jnp.mean(centered * centered, axis=-1, keepdims=True)
    return centered * lax.rsqrt(spread + EPS)


def kernel(
    x_in, gain1, gain2, qkv1, out1, up1, down1, qkv2, out2, up2, down2,
    y_out,
    w, xs, h, terms, from_x, to_z, from_z, mid, turned,
    local_sem, w_send, w_recv, ag_send, ag_recv, rx_send, rx_recv, rz_send, rz_recv, turn_send, turn_recv,
):
    f, t = lax.axis_index("frame"), lax.axis_index("tensor")
    xi, zh = t // 4, t % 4
    f_z = (f // 4) * 4 + (f + 2) % 4
    f_core = f + 1 - 2 * (f % 2)
    f_up, f_down = (f + 4) % 32, (f + 28) % 32

    def tensor_at(dx, dz):
        return ((xi + dx) % 4) * 4 + (zh + dz) % 4

    pending = []

    def send(src, dst, send_sem, recv_sem, device):
        copy = pltpu.make_async_remote_copy(src, dst, send_sem, recv_sem, device_id=device, device_id_type=MESH)
        copy.start()
        pending.append(copy)

    def arrived(dst, recv_sem):
        pltpu.make_async_remote_copy(dst, dst, recv_sem, recv_sem, device_id=(f_core, t), device_id_type=MESH).wait_recv()

    local = [pltpu.make_async_copy(x_in, xs.at[0, t], local_sem.at[12])]
    for b, (qkv, up, out, down) in enumerate(((qkv1, up1, out1, down1), (qkv2, up2, out2, down2))):
        parts = [(qkv.at[j], 128 * j, 128) for j in range(3)] + [(up, 384, 256), (out, 640, 128), (down, 768, 256)]
        for i, (ref, at, width) in enumerate(parts):
            local.append(pltpu.make_async_copy(ref, w.at[b, f, :, pl.ds(at, width)], local_sem.at[6 * b + i]))
    for copy in local:
        copy.start()

    barrier = pltpu.get_barrier_semaphore()
    peers = [(f_z, t), (f_core, t), (f_up, t), (f_down, t)]
    peers += [(f, tensor_at(dx, 0)) for dx in (1, 2, 3)] + [(f, tensor_at(0, dz)) for dz in (1, 2, 3)]
    for peer in peers:
        pl.semaphore_signal(barrier, inc=1, device_id=peer, device_id_type=MESH)
    for copy in local:
        copy.wait()
    pl.semaphore_wait(barrier, len(peers))

    used = [0, 0]

    def w_push(b, slot, target):
        send(w.at[b, slot], w.at[b, slot], w_send.at[b, used[b]], w_recv.at[b, slot], (target, t))
        used[b] += 1

    def w_wait(b, slot):
        arrived(w.at[b, slot], w_recv.at[b, slot])

    def w_own(b):
        w_push(b, f, f_z)
        w_push(b, f, f_up)
        w_push(b, f, f_down)
        w_push(b, f, f_core)

    def w_pair(b):
        w_wait(b, f_z)
        w_push(b, f_z, f_up)
        w_push(b, f_z, f_down)
        w_push(b, f_z, f_core)

    def w_hop(b, hop):
        below = [(f + 32 - 4 * hop) % 32, (f_z + 32 - 4 * hop) % 32]
        above = [(f + 4 * hop) % 32, (f_z + 4 * hop) % 32]
        for i in range(2):
            w_wait(b, below[i])
            if hop < 3 or i == 0:
                w_push(b, below[i], f_up)
            w_push(b, below[i], f_core)
            w_wait(b, above[i])
            if hop < 3 or i == 1:
                w_push(b, above[i], f_down)
            w_push(b, above[i], f_core)

    def w_last(b):
        for slot in ((f + 16) % 32, (f_z + 16) % 32):
            w_wait(b, slot)
            w_push(b, slot, f_core)

    def w_core(b):
        for k in range(8):
            w_wait(b, (f_core + 4 * k) % 32)
            w_wait(b, (f_core // 4 * 4 + (f_core + 2) % 4 + 4 * k) % 32)

    def gather_push(b, dx, dz, to_dx, to_dz):
        slot = tensor_at(4 - dx, 4 - dz)
        rel = (dx + to_dx) * 4 + dz + to_dz
        send(xs.at[b, slot], xs.at[b, slot], ag_send.at[b, rel], ag_recv.at[b, rel], (f, tensor_at(to_dx, to_dz)))

    def gather_wait(b, dx, dz):
        arrived(xs.at[b, tensor_at(4 - dx, 4 - dz)], ag_recv.at[b, dx * 4 + dz])

    def gather_own(b):
        for dz in (2, 1, 3):
            gather_push(b, 0, 0, 0, dz)
        for dx in (2, 1, 3):
            gather_push(b, 0, 0, dx, 0)

    def gather_forward(b, dz):
        gather_wait(b, 0, dz)
        for dx in (2, 1, 3):
            gather_push(b, 0, dz, dx, 0)

    def gather_rest(b):
        for dz in (0, 1, 3, 2):
            for dx in (1, 2, 3):
                gather_wait(b, dx, dz)

    def normalize(b):
        total = xs[b, 0].astype(F32)
        for i in range(1, 16):
            total += xs[b, i].astype(F32)
        mean = jnp.sum(total, axis=-1, keepdims=True) * (1.0 / 2048)
        square = jnp.zeros((256, 128), F32)
        for i in range(16):
            centered = xs[b, i].astype(F32) - mean
            square += centered * centered
        scale = lax.rsqrt(jnp.sum(square, axis=-1, keepdims=True) * (1.0 / 2048) + EPS)
        for i in range(16):
            centered = xs[b, i].astype(F32) - mean
            h[:, 128 * i : 128 * (i + 1)] = (centered * scale * (gain1, gain2)[b][i]).astype(BF)

    def inner(b):
        mixed = jnp.dot(h[...], w[b, :, :, 0:640].reshape(2048, 640), preferred_element_type=F32)
        query = norm_rows(mixed[:, 0:128]).astype(BF)
        keys = norm_rows(mixed[:, 128:256]).astype(BF)
        scores = lax.dot_general(query, keys, NT, preferred_element_type=F32) * 128**-0.5
        expo = jnp.exp(scores)
        if b == 1:
            row = lax.broadcasted_iota(jnp.int32, (256, 256), 0)
            col = lax.broadcasted_iota(jnp.int32, (256, 256), 1)
            expo = jnp.where(row % 8 == col % 8, expo, 0.0)
        weights = (expo * (1.0 / jnp.sum(expo, axis=-1, keepdims=True))).astype(BF)
        attended = jnp.dot(weights, mixed[:, 256:384].astype(BF), preferred_element_type=F32).astype(BF)
        hidden = jax.nn.gelu(mixed[:, 384:640], approximate=True).astype(BF)
        return jnp.concatenate([attended, hidden], axis=1)

    order = (2, 1, 3, 0)

    def project(b, both):
        for dz in order:
            for dx in (2, 1, 3, 0):
                slot = 2 * tensor_at(dx, dz)
                piece = w[b, pl.ds(slot, 2), :, 640:1024].reshape(128, 384)
                terms[b, dx, dz] = lax.dot_general(both, piece, NT, preferred_element_type=F32).astype(BF)
                if dx:
                    send(
                        terms.at[b, dx, dz], from_x.at[b, dx - 1, dz], rx_send.at[b, dx - 1, dz],
                        rx_recv.at[b, dx - 1, dz], (f, tensor_at(dx, 0)),
                    )

    def reduce(b):
        total = None
        for dz in order:
            total = terms[b, 0, dz].astype(F32)
            for i in range(3):
                arrived(from_x.at[b, i, dz], rx_recv.at[b, i, dz])
                total += from_x[b, i, dz].astype(F32)
            if dz:
                to_z[b, dz - 1] = total.astype(BF)
                send(
                    to_z.at[b, dz - 1], from_z.at[b, dz - 1], rz_send.at[b, dz - 1], rz_recv.at[b, dz - 1],
                    (f, tensor_at(0, dz)),
                )
        for i in (0, 2, 1):
            arrived(from_z.at[b, i], rz_recv.at[b, i])
            total += from_z[b, i].astype(F32)
        return total

    def turn(middle):
        mid[...] = middle.reshape(32, 8, 128)
        for i in range(1, 32):
            to = (f + i) % 32
            send(mid.at[to], turned.at[f], turn_send.at[i - 1], turn_recv.at[i - 1], (to, t))
        turned[f] = mid[f]
        for i in range(1, 32):
            arrived(turned.at[(f + 32 - i) % 32], turn_recv.at[i - 1])

    gather_own(0)
    w_own(0)
    w_pair(0)
    for dz in (1, 3, 2):
        gather_forward(0, dz)
    w_hop(0, 1)
    w_hop(0, 2)
    w_hop(0, 3)
    w_own(1)
    gather_rest(0)
    normalize(0)
    w_last(0)
    w_pair(1)
    w_core(0)
    both = inner(0)
    project(0, both)
    w_hop(1, 1)
    share = reduce(0)
    middle = (xs[0, t].astype(F32) + share).astype(BF).astype(F32)
    turn(middle)
    xs[1, t] = turned[...].reshape(256, 128).astype(BF)
    gather_own(1)
    w_hop(1, 2)
    for dz in (1, 3, 2):
        gather_forward(1, dz)
    w_hop(1, 3)
    w_last(1)
    gather_rest(1)
    normalize(1)
    w_core(1)
    both = inner(1)
    project(1, both)
    share = reduce(1)
    y_out[...] = (turned[...].reshape(256, 128) + share).astype(BF)
    for copy in pending:
        copy.wait_send()


def body(
    frames_in,
    spatial_gain,
    spatial_qkv,
    spatial_out,
    spatial_up,
    spatial_down,
    temporal_gain,
    temporal_qkv,
    temporal_out,
    temporal_up,
    temporal_down,
):
    dma = pltpu.SemaphoreType.DMA
    result = pl.pallas_call(
        kernel,
        out_shape=jax.ShapeDtypeStruct((256, 128), BF),
        in_specs=[pl.BlockSpec(memory_space=pl.ANY), pl.BlockSpec(memory_space=pltpu.VMEM), pl.BlockSpec(memory_space=pltpu.VMEM)]
        + [pl.BlockSpec(memory_space=pl.ANY)] * 8,
        out_specs=pl.BlockSpec(memory_space=pltpu.VMEM),
        scratch_shapes=[
            pltpu.VMEM((2, 32, 64, 1024), BF),
            pltpu.VMEM((2, 16, 256, 128), BF),
            pltpu.VMEM((256, 2048), BF),
            pltpu.VMEM((2, 4, 4, 256, 128), BF),
            pltpu.VMEM((2, 3, 4, 256, 128), BF),
            pltpu.VMEM((2, 3, 256, 128), BF),
            pltpu.VMEM((2, 3, 256, 128), BF),
            pltpu.VMEM((32, 8, 128), F32),
            pltpu.VMEM((32, 8, 128), F32),
            dma((13,)),
            dma((2, 31)),
            dma((2, 32)),
            dma((2, 16)),
            dma((2, 16)),
            dma((2, 3, 4)),
            dma((2, 3, 4)),
            dma((2, 3)),
            dma((2, 3)),
            dma((31,)),
            dma((31,)),
        ],
        compiler_params=pltpu.CompilerParams(collective_id=0, has_side_effects=True, vmem_limit_bytes=63 << 20),
    )(
        frames_in.reshape(256, 128),
        spatial_gain.reshape(16, 1, 128),
        temporal_gain.reshape(16, 1, 128),
        jnp.transpose(spatial_qkv, (1, 0, 2)),
        spatial_out,
        spatial_up,
        spatial_down,
        jnp.transpose(temporal_qkv, (1, 0, 2)),
        temporal_out,
        temporal_up,
        temporal_down,
    )
    return result.reshape(32, 8, 128)


def solution(mesh):
    in_specs = (
        P("frame", None, "tensor"),
        P(),
        P("frame", None, "tensor"),
        P("frame", "tensor"),
        P("frame", "tensor"),
        P("frame", "tensor"),
        P(),
        P("frame", None, "tensor"),
        P("frame", "tensor"),
        P("frame", "tensor"),
        P("frame", "tensor"),
    )
    out_specs = P(None, "frame", "tensor")
    return jax.shard_map(body, mesh=mesh, in_specs=in_specs, out_specs=out_specs, check_vma=False)
```

time: 820 us -> 113 us (0.14)
  waiting for transfers between devices: 598 us -> 0 us
  Pallas kernels: 0 us -> 110 us
  blocking collectives: 100 us -> 0 us
  local copies, waits for them, and re-layouts: 60.4 us -> 1.47 us
  starting transfers between devices: 18.6 us -> 0 us
  other arithmetic: 14.2 us -> 0 us
  matrix products: 13.9 us -> 0 us
  between operations: 13.5 us -> 0.01 us
    all_gather x7 -> x0, waiting for transfers between devices: 339 us -> none  [the longest x2 137 us: branch_terms(): lax.all_gather((out_weight, down_weight), 'frame', axis=0, tiled=True)]
    psum x1 -> x0, waiting for transfers between devices: 164 us -> none  [body(): lax.psum(partial_value.astype(jnp.bfloat16), 'tensor').astype(jnp.float32)]
    pallas_call x0 -> x1, Pallas kernels: none -> 110 us  [body(): pl.pallas_call(kernel, out_shape=jax.ShapeDtypeStruct((256, 128), BF), in...]
    all_gather x2 -> x0, blocking collectives: 100 us -> none  [branch_terms(): lax.all_gather((out_weight, down_weight), 'frame', axis=0, tiled=True)]
    unnamed x10 -> x0, waiting for transfers between devices: 94.2 us -> none
    unnamed x19 -> x1, local copies, waits for them, and re-layouts: 54.4 us -> 1.47 us
    all_to_all x1 -> x0, starting transfers between devices: 18.1 us -> none  [body(): lax.all_to_all(middle, 'frame', split_axis=1, concat_axis=0, tiled=True)]
    dot_general x9 -> x0, matrix products: 13.9 us -> none  [the longest x2 7.76 us: branch_terms(): lax.dot_general(hidden, pieces[1], contract, preferred_element_type=jnp.f...]
  transfers between devices with their start and end apart: 10 -> 0, of which waited for: 8 -> 0; matrix products, arithmetic and copies ran while one was open for 4% -> 0% of each run, Pallas kernels for 0% -> 0%
where the time goes in v1:
time: 113 us; the launch traced here: 111 us
  Pallas kernels  110 us (97%)
  local copies, waits for them, and re-layouts  1.47 us (1%)
    pallas_call x1, Pallas kernels, body(): pl.pallas_call(kernel, out_shape=jax.ShapeDtypeStruct((256, 128), BF), in...  110 us

profile of v1, /device:TPU:1, one launch (start us, length us, event | category | flops | bytes accessed | tf_op | source)
XLA Modules:
  0.0 111.2 jit_solution(15632628355609300958)
XLA Ops:
  0.0 109.8 %shard_map.109 = bf16[256,128]{1,0:T(8,128)(2,1)} custom-call(bf16[256,128]{1,0:T(8,128)(2,1)} %bitcast.7, f32[16,1,128]{2,1,0:T(1,128)} %bitcast.10, f32[16,1,128]{2,1,0:T(1,128)} %bitcast.11, bf16[3,64,128]{2,1,0:T(8,128)(2,1)} %bitcast.8, bf16[64,128]{1,0:T(8,128)(2,1)} %out1.1, bf16[64,256]{1,0:T(8,128)(2,1)} %up1.1, bf16[64,256]{1,0:T(8,128)(2,1)} %down1.1, ...), custom_call_target="tpu_custom_call" | custom-call | tf_op jit(solution)/shard_map/pallas_call | solution.py:253
  109.8 1.5 %copy.13 = bf16[32,8,128]{2,1,0:T(8,128)(2,1)} copy(bf16[32,8,128]{2,1,0:T(8,128)(2,1)} %bitcast.6) | data formatting | bytes 131072

commit v2 on v0

v2 whole, which is shorter than its diff:
```python
import jax
import jax.numpy as jnp
from jax import lax
from jax.experimental import pallas as pl
from jax.experimental.pallas import tpu as pltpu
from jax.sharding import PartitionSpec as P

MESH = pl.DeviceIdType.MESH
EPS = 1e-06
BF = jnp.bfloat16
F32 = jnp.float32
NT = (((1,), (1,)), ((), ()))
PARTS = 2
EACH = 8 // PARTS
ROWS = 32 * EACH
EACH_BITS, ROWS_BITS = EACH.bit_length() - 1, ROWS.bit_length() - 1
PIECES = (4, 2)


def norm_rows(values):
    centered = values - jnp.mean(values, axis=-1, keepdims=True)
    spread = jnp.mean(centered * centered, axis=-1, keepdims=True)
    return centered * lax.rsqrt(spread + EPS)


def kernel(
    x_in, gain1_in, gain2_in, qkv1, out1, up1, down1, qkv2, out2, up2, down2,
    y_out,
    w, gain1, gain2, x_own, xs, xt, h, terms, from_x, to_z, from_z, mid, turned, ready,
    local_sem, w_send, w_early, w_late, w_last, ag_send, ag_recv, rx_send, rx_recv, rz_send, rz_recv, turn_send, turn_recv,
):
    f, t = lax.axis_index("frame"), lax.axis_index("tensor")
    xi, zh = t // 4, t % 4
    odd, lo = f % 2, (f // 2) % 2
    f_z = (f // 4) * 4 + (f + 2) % 4
    f_core = f + 1 - 2 * odd

    def at_y(base, r):
        return (base + 4 * (r % 8)) % 32

    def tensor_at(dx, dz):
        return ((xi + dx) % 4) * 4 + (zh + dz) % 4

    def send(src, dst, send_sem, recv_sem, device):
        pltpu.make_async_remote_copy(src, dst, send_sem, recv_sem, device_id=device, device_id_type=MESH).start()

    def arrived(ref, sem):
        pltpu.make_async_remote_copy(ref, ref, sem, sem, device_id=(f_core, t), device_id_type=MESH).wait_recv()

    def left(ref, sem):
        pltpu.make_async_remote_copy(ref, ref, sem, sem, device_id=(f_core, t), device_id_type=MESH).wait_send()

    def part_order(axis):
        shapes = [(256, 1), (1, 256)]
        part = lax.broadcasted_iota(jnp.int32, shapes[axis], axis)
        own = lax.broadcasted_iota(jnp.int32, shapes[1 - axis], 1 - axis)
        natural = ((part & (ROWS - 1)) >> EACH_BITS << 3) + (part >> ROWS_BITS << EACH_BITS) + (part & (EACH - 1))
        return jnp.where(natural == own, 1.0, 0.0).astype(BF)

    pltpu.make_async_copy(x_in, x_own, local_sem.at[0]).start()
    pltpu.make_async_copy(gain1_in, gain1, local_sem.at[1]).start()
    pltpu.make_async_copy(gain2_in, gain2, local_sem.at[2]).start()
    for b, (qkv, up, out, down) in enumerate(((qkv1, up1, out1, down1), (qkv2, up2, out2, down2))):
        for ref, at, width in [(qkv.at[j], 128 * j, 128) for j in range(3)] + [(up, 384, 256), (out, 640, 128), (down, 768, 256)]:
            pltpu.make_async_copy(ref, w.at[b, f, :, pl.ds(at, width)], local_sem.at[3 + b]).start()

    def placed(ref, k):
        pltpu.make_async_copy(ref, ref, local_sem.at[k]).wait()

    barrier = pltpu.get_barrier_semaphore()
    peers = [(f_z, t), (f_core, t), (at_y(f, 1), t), (at_y(f, -1), t)]
    peers += [(f, tensor_at(dx, 0)) for dx in (1, 2, 3)] + [(f, tensor_at(0, dz)) for dz in (1, 2, 3)]
    for peer in peers:
        pl.semaphore_signal(barrier, inc=1, device_id=peer, device_id_type=MESH)
    placed(x_own, 0)
    placed(w.at[0, f], 3)
    xs[t] = jnp.dot(part_order(0), x_own[...], preferred_element_type=F32).astype(BF)
    pl.semaphore_wait(barrier, len(peers))

    used = [0, 0]

    def piece(b, i, slot):
        rows = 64 // PIECES[b]
        return w.at[b, slot, pl.ds(i * rows, rows), :]

    def w_sem(b, i, kind):
        return w_late.at[i, kind] if b else w_early.at[i, kind]

    def w_push(b, i, slot, target, kind=None):
        used[b] += 1
        send(piece(b, i, slot), piece(b, i, slot), w_send.at[b], w_last.at[b] if kind is None else w_sem(b, i, kind), (target, t))

    def w_first(b, i):
        w_push(b, i, f, f_z, 4)
        w_push(b, i, f, at_y(f, 1), 0)
        w_push(b, i, f, at_y(f, -1), 0)
        w_push(b, i, f, f_core)

    def w_rank(b, i, own, k):
        base = f if own else f_z
        early = i < PIECES[b] // 2
        kind = k - 1 if own else 4 + k
        rows = 64 // PIECES[b]
        both = k in (1, 2, 3)
        arrived(w.at[b, pl.ds(0, 2), pl.ds(0, rows), :] if both else piece(b, i, at_y(base, k)), w_sem(b, i, kind))
        for r in (-k, k) if both else (k,):
            slot = at_y(base, r)
            if own or early:
                if r in (-2, -1, 0):
                    w_push(b, i, slot, at_y(f, 1), kind + 1)
                if r in (0, 1, 2):
                    w_push(b, i, slot, at_y(f, -1), kind + 1)
                if early and r == (-3 if own else 3):
                    w_push(b, i, slot, at_y(f, 1 if own else -1), kind + 1)
            if own and not early:
                if r == 3:
                    w_push(b, i, at_y(f, -3 + 6 * odd), at_y(f, 1 - 2 * odd), kind + 1)
                w_push(b, i, slot, f_z, 4 + k)
            w_push(b, i, slot, f_core)

    def w_core(b):
        arrived(w.at[b, pl.ds(0, 16)], w_last.at[b])

    def gather_push(view, k, dx, dz, to_dx, to_dz):
        slot = view.at[tensor_at(4 - dx, 4 - dz)]
        send(slot, slot, ag_send.at[k], ag_recv.at[k, to_dz], (f, tensor_at(to_dx, to_dz)))

    def gather_own(view, k):
        for dz in (2, 1, 3):
            gather_push(view, k, 0, 0, 0, dz)
        for dx in (2, 1, 3):
            gather_push(view, k, 0, 0, dx, 0)

    def gather_forward(view, k, dz):
        arrived(view.at[tensor_at(0, 4 - dz)], ag_recv.at[k, dz])
        for dx in (2, 1, 3):
            gather_push(view, k, 0, dz, dx, 0)

    def gather_rest(view, k):
        arrived(view.at[pl.ds(0, 12)], ag_recv.at[k, 0])

    def normalize(view, rows, gain):
        total = view[0].astype(F32)
        for i in range(1, 16):
            total += view[i].astype(F32)
        mean = jnp.sum(total, axis=-1, keepdims=True) * (1.0 / 2048)
        square = jnp.zeros((rows, 128), F32)
        for i in range(16):
            centered = view[i].astype(F32) - mean
            square += centered * centered
        scale = lax.rsqrt(jnp.sum(square, axis=-1, keepdims=True) * (1.0 / 2048) + EPS)
        for i in range(16):
            centered = view[i].astype(F32) - mean
            h[0:rows, 128 * i : 128 * (i + 1)] = (centered * scale * gain[i]).astype(BF)

    def inner(b, rows):
        mixed = jnp.dot(h[0:rows, :], w[b, :, :, 0:640].reshape(2048, 640), preferred_element_type=F32)
        query = norm_rows(mixed[:, 0:128]).astype(BF)
        keys = norm_rows(mixed[:, 128:256]).astype(BF)
        scores = lax.dot_general(query, keys, NT, preferred_element_type=F32) * 128**-0.5
        expo = jnp.exp(scores)
        if b == 1:
            row = lax.broadcasted_iota(jnp.int32, (rows, 1), 0)
            col = lax.broadcasted_iota(jnp.int32, (1, rows), 1)
            expo = jnp.where((row & (EACH - 1)) == (col & (EACH - 1)), expo, 0.0)
        weights = (expo * (1.0 / jnp.sum(expo, axis=-1, keepdims=True))).astype(BF)
        attended = jnp.dot(weights, mixed[:, 256:384].astype(BF), preferred_element_type=F32).astype(BF)
        hidden = jax.nn.gelu(mixed[:, 384:640], approximate=True).astype(BF)
        return jnp.concatenate([attended, hidden], axis=1)

    order = (2, 1, 3, 0)

    groups = []

    def project(b, k, dz, both):
        n = len(groups)
        if n >= 2:
            left(from_x.at[0, 0, 0], rx_send.at[n % 2])
        for dx in (2, 1, 3, 0):
            slot = 2 * tensor_at(dx, dz)
            weight = w[b, pl.ds(slot, 2), :, 640:1024].reshape(128, 384)
            terms[b, k, dx, dz] = lax.dot_general(both, weight, NT, preferred_element_type=F32).astype(BF)
            if dx:
                send(terms.at[b, k, dx, dz], from_x.at[b, k, dz, dx - 1], rx_send.at[n % 2], rx_recv.at[b, k, dz], (f, tensor_at(dx, 0)))
        groups.append(n)

    def sum_x(b, k, dz):
        arrived(from_x.at[b, k, dz], rx_recv.at[b, k, dz])
        total = terms[b, k, 0, dz].astype(F32)
        for i in range(3):
            total += from_x[b, k, dz, i].astype(F32)
        if dz:
            to_z[b, k, dz - 1] = total.astype(BF)
            send(to_z.at[b, k, dz - 1], from_z.at[b, k, dz - 1], rz_send.at[0], rz_recv.at[b, k], (f, tensor_at(0, dz)))
        else:
            ready[b, k] = total

    def sum_z(b, k):
        arrived(from_z.at[b, k], rz_recv.at[b, k])
        total = ready[b, k]
        for i in range(3):
            total += from_z[b, k, i].astype(F32)
        return total

    distances = sorted(range(1, 32), key=lambda i: -min(i // 4, 8 - i // 4))

    def turn(k):
        middle = (xs[t, k * ROWS : (k + 1) * ROWS, :].astype(F32) + sum_z(0, k)).astype(BF).astype(F32)
        mid[k] = middle.reshape(32, EACH, 128)
        for i in distances:
            to = (f + i) % 32
            send(mid.at[k, to], turned.at[k, f], turn_send.at[k], turn_recv.at[k], (to, t))
        turned[k, f] = mid[k, f]

    def turn_done(k):
        arrived(turned.at[k, pl.ds(0, 31)], turn_recv.at[k])
        xt[k, t] = turned[k].reshape(ROWS, 128).astype(BF)

    quarters = range(PIECES[0])
    for i in quarters[:1]:
        w_first(0, i)
    gather_own(xs, 0)
    for i in quarters[1:]:
        w_first(0, i)
    for i in quarters:
        w_rank(0, i, True, 1)
    for i in quarters:
        w_rank(0, i, False, 0)
    for i in (0, 1):
        w_rank(0, i, True, 2)
    gather_forward(xs, 0, 3 - 2 * lo)
    for i in (2, 3):
        w_rank(0, i, True, 2)
    for i in quarters:
        w_rank(0, i, False, 1)
    for i in (0, 1):
        w_rank(0, i, True, 3)
    gather_forward(xs, 0, 1 + 2 * lo)
    w_rank(0, 2, True, 3)
    gather_forward(xs, 0, 2)
    w_rank(0, 2, False, 2)
    w_rank(0, 3, True, 3)
    w_rank(0, 3, False, 2)
    for i in (0, 1):
        w_rank(0, i, False, 2)
    for i in quarters:
        w_rank(0, i, True, 4)
    for i in (2, 3, 0, 1):
        w_rank(0, i, False, 3)
    w_rank(0, 2, False, 4)
    gather_rest(xs, 0)
    placed(gain1, 1)
    normalize(xs, 256, gain1)
    for i in (3, 0, 1):
        w_rank(0, i, False, 4)

    def second(k):
        for i in range(PIECES[1]):
            if 0 < k < 5:
                w_rank(1, i, True, k)
            if k > 0:
                w_rank(1, i, False, k - 1)
            else:
                w_first(1, i)

    blocks = [(k, dz) for k in range(PARTS) for dz in order]

    def branch(b, rows_of, after_sum):
        issued = 0
        for i, (k, dz) in enumerate(blocks):
            for ahead in blocks[issued : i + 4]:
                project(b, *ahead, rows_of(*ahead))
                issued += 1
            sum_x(b, k, dz)
            after_sum(k, dz)

    w_core(0)
    both = inner(0, 256)
    placed(w.at[1, f], 4)
    placed(gain2, 2)
    second(0)

    def turn_last(k, dz):
        if k and dz == order[1]:
            turn(k - 1)

    branch(0, lambda k, dz: both[k * ROWS : (k + 1) * ROWS], turn_last)
    second(1)
    turn(PARTS - 1)
    for k in range(PARTS):
        turn_done(k)
        gather_own(xt.at[k], k + 1)
        if k == 0:
            second(2)
    for k in range(PARTS):
        for dz in (1, 3, 2):
            gather_forward(xt.at[k], k + 1, dz)
        if k == 0:
            second(3)
            second(4)

    rows2 = {}

    def enter(k, dz):
        if k not in rows2:
            gather_rest(xt.at[k], k + 1)
            normalize(xt.at[k], ROWS, gain2)
            if k == 0:
                second(5)
                w_core(1)
            rows2[k] = inner(1, ROWS)
        return rows2[k]

    branch(1, enter, lambda k, dz: None)
    total = jnp.concatenate([sum_z(1, k) for k in range(PARTS)], axis=0)
    kept = jnp.concatenate([turned[k].reshape(ROWS, 128) for k in range(PARTS)], axis=0)
    y_out[...] = jnp.dot(part_order(1), (kept + total).astype(BF), preferred_element_type=F32).astype(BF)
    for b in range(2):
        left(w.at[b, pl.ds(0, used[b] // PIECES[b])], w_send.at[b])
        left(from_x.at[0, 0, 0], rx_send.at[b])
    left(xs.at[pl.ds(0, 15)], ag_send.at[0])
    for k in range(PARTS):
        left(xt.at[k, pl.ds(0, 15)], ag_send.at[k + 1])
        left(mid.at[k, pl.ds(0, 31)], turn_send.at[k])
    left(to_z, rz_send.at[0])


def body(
    frames_in,
    spatial_gain,
    spatial_qkv,
    spatial_out,
    spatial_up,
    spatial_down,
    temporal_gain,
    temporal_qkv,
    temporal_out,
    temporal_up,
    temporal_down,
):
    dma = pltpu.SemaphoreType.DMA
    result = pl.pallas_call(
        kernel,
        out_shape=jax.ShapeDtypeStruct((256, 128), BF),
        in_specs=[pl.BlockSpec(memory_space=pl.ANY)] * 11,
        out_specs=pl.BlockSpec(memory_space=pltpu.VMEM),
        scratch_shapes=[
            pltpu.VMEM((2, 32, 64, 1024), BF),
            pltpu.VMEM((16, 1, 128), F32),
            pltpu.VMEM((16, 1, 128), F32),
            pltpu.VMEM((256, 128), BF),
            pltpu.VMEM((16, 256, 128), BF),
            pltpu.VMEM((PARTS, 16, ROWS, 128), BF),
            pltpu.VMEM((256, 2048), BF),
            pltpu.VMEM((2, PARTS, 4, 4, ROWS, 128), BF),
            pltpu.VMEM((2, PARTS, 4, 3, ROWS, 128), BF),
            pltpu.VMEM((2, PARTS, 3, ROWS, 128), BF),
            pltpu.VMEM((2, PARTS, 3, ROWS, 128), BF),
            pltpu.VMEM((PARTS, 32, EACH, 128), F32),
            pltpu.VMEM((PARTS, 32, EACH, 128), F32),
            pltpu.VMEM((2, PARTS, ROWS, 128), F32),
            dma((5,)),
            dma((2,)),
            dma((PIECES[0], 9)),
            dma((PIECES[1], 9)),
            dma((2,)),
            dma((1 + PARTS,)),
            dma((1 + PARTS, 4)),
            dma((2,)),
            dma((2, PARTS, 4)),
            dma((1,)),
            dma((2, PARTS)),
            dma((PARTS,)),
            dma((PARTS,)),
        ],
        compiler_params=pltpu.CompilerParams(collective_id=0, has_side_effects=True, vmem_limit_bytes=63 << 20),
    )(
        frames_in.reshape(256, 128),
        spatial_gain.reshape(16, 1, 128),
        temporal_gain.reshape(16, 1, 128),
        jnp.transpose(spatial_qkv, (1, 0, 2)),
        spatial_out,
        spatial_up,
        spatial_down,
        jnp.transpose(temporal_qkv, (1, 0, 2)),
        temporal_out,
        temporal_up,
        temporal_down,
    )
    return result.reshape(32, 8, 128)


def solution(mesh):
    in_specs = (
        P("frame", None, "tensor"),
        P(),
        P("frame", None, "tensor"),
        P("frame", "tensor"),
        P("frame", "tensor"),
        P("frame", "tensor"),
        P(),
        P("frame", None, "tensor"),
        P("frame", "tensor"),
        P("frame", "tensor"),
        P("frame", "tensor"),
    )
    out_specs = P(None, "frame", "tensor")
    return jax.shard_map(body, mesh=mesh, in_specs=in_specs, out_specs=out_specs, check_vma=False)
```

time: 820 us -> 96.1 us (0.12)
  waiting for transfers between devices: 598 us -> 0 us
  blocking collectives: 100 us -> 0 us
  Pallas kernels: 0 us -> 94.4 us
  local copies, waits for them, and re-layouts: 60.4 us -> 1.47 us
  starting transfers between devices: 18.6 us -> 0 us
  other arithmetic: 14.2 us -> 0 us
  matrix products: 13.9 us -> 0 us
  between operations: 13.5 us -> 0.01 us
    all_gather x7 -> x0, waiting for transfers between devices: 339 us -> none  [the longest x2 137 us: branch_terms(): lax.all_gather((out_weight, down_weight), 'frame', axis=0, tiled=True)]
    psum x1 -> x0, waiting for transfers between devices: 164 us -> none  [body(): lax.psum(partial_value.astype(jnp.bfloat16), 'tensor').astype(jnp.float32)]
    all_gather x2 -> x0, blocking collectives: 100 us -> none  [branch_terms(): lax.all_gather((out_weight, down_weight), 'frame', axis=0, tiled=True)]
    pallas_call x0 -> x1, Pallas kernels: none -> 94.4 us  [body(): pl.pallas_call(kernel, out_shape=jax.ShapeDtypeStruct((256, 128), BF), in...]
    unnamed x10 -> x0, waiting for transfers between devices: 94.2 us -> none
    unnamed x19 -> x1, local copies, waits for them, and re-layouts: 54.4 us -> 1.47 us
    all_to_all x1 -> x0, starting transfers between devices: 18.1 us -> none  [body(): lax.all_to_all(middle, 'frame', split_axis=1, concat_axis=0, tiled=True)]
    dot_general x9 -> x0, matrix products: 13.9 us -> none  [the longest x2 7.76 us: branch_terms(): lax.dot_general(hidden, pieces[1], contract, preferred_element_type=jnp.f...]
  transfers between devices with their start and end apart: 10 -> 0, of which waited for: 8 -> 0; matrix products, arithmetic and copies ran while one was open for 4% -> 0% of each run, Pallas kernels for 0% -> 0%
where the time goes in v2:
time: 96.1 us; the launch traced here: 95.9 us
  Pallas kernels  94.4 us (98%)
  local copies, waits for them, and re-layouts  1.47 us (2%)
    pallas_call x1, Pallas kernels, body(): pl.pallas_call(kernel, out_shape=jax.ShapeDtypeStruct((256, 128), BF), in...  94.4 us

profile of v2, /device:TPU:1, one launch (start us, length us, event | category | flops | bytes accessed | tf_op | source)
XLA Modules:
  0.0 95.9 jit_solution(2162831705716585527)
XLA Ops:
  0.0 94.4 %shard_map.109 = bf16[256,128]{1,0:T(8,128)(2,1)} custom-call(bf16[256,128]{1,0:T(8,128)(2,1)} %bitcast.7, f32[16,1,128]{2,1,0:T(1,128)} %bitcast.10, f32[16,1,128]{2,1,0:T(1,128)} %bitcast.11, bf16[3,64,128]{2,1,0:T(8,128)(2,1)} %bitcast.8, bf16[64,128]{1,0:T(8,128)(2,1)} %out1.1, bf16[64,256]{1,0:T(8,128)(2,1)} %up1.1, bf16[64,256]{1,0:T(8,128)(2,1)} %down1.1, ...), custom_call_target="tpu_custom_call" | custom-call | tf_op jit(solution)/shard_map/pallas_call | solution.py:342
  94.4 1.5 %copy.13 = bf16[32,8,128]{2,1,0:T(8,128)(2,1)} copy(bf16[32,8,128]{2,1,0:T(8,128)(2,1)} %bitcast.6) | data formatting | bytes 131072

commit v3 on v2

--- a/solution.py
+++ b/solution.py
@@ -15,6 +15,33 @@
 ROWS = 32 * EACH
 EACH_BITS, ROWS_BITS = EACH.bit_length() - 1, ROWS.bit_length() - 1
 PIECES = (4, 2)
+
+PLAN = (
+    ("project", 0, 0, 2), ("first",), ("project", 0, 0, 1), ("project", 0, 0, 3), ("project", 0, 0, 0),
+    ("weight", 0, False, 0), ("project", 0, 1, 2), ("sum", 0, 0, 2), ("project", 0, 1, 1), ("weight", 1, True, 1),
+    ("sum", 0, 0, 1), ("project", 0, 1, 3), ("sum", 0, 0, 3), ("weight", 0, False, 1), ("project", 0, 1, 0),
+    ("weight", 1, False, 0), ("sum", 0, 1, 2), ("sum", 0, 0, 0), ("sum", 0, 1, 1), ("sum", 0, 1, 3), ("turn", 0),
+    ("sum", 0, 1, 0), ("weight", 0, True, 1), ("turn", 1), ("weight", 0, True, 2), ("turned", 0), ("weight", 1, False, 1),
+    ("weight", 1, True, 2), ("turned", 1), ("weight", 0, False, 2), ("forward", 0, 3), ("weight", 1, False, 2),
+    ("forward", 0, 2), ("forward", 0, 1), ("weight", 0, True, 3), ("weight", 0, False, 3), ("weight", 1, True, 3),
+    ("weight", 1, False, 3), ("forward", 1, 3), ("weight", 0, True, 4), ("forward", 1, 2), ("forward", 1, 1),
+    ("weight", 1, True, 4), ("weight", 0, False, 4), ("weight", 1, False, 4), ("enter", 0), ("project", 1, 0, 2),
+    ("project", 1, 0, 1), ("project", 1, 0, 3), ("enter", 1), ("project", 1, 1, 2), ("project", 1, 1, 1), ("sum", 1, 0, 2),
+    ("project", 1, 1, 3), ("sum", 1, 0, 1), ("sum", 1, 0, 3), ("sum", 1, 1, 2), ("project", 1, 0, 0), ("project", 1, 1, 0),
+    ("sum", 1, 1, 1), ("sum", 1, 1, 3), ("sum", 1, 0, 0), ("sum", 1, 1, 0),
+)
+PLAN_FIRST = (
+    ("weight", 0, True, 1), ("weight", 1, True, 1), ("weight", 0, False, 0), ("weight", 1, False, 0),
+    ("weight", 2, False, 0), ("weight", 2, True, 1), ("weight", 0, True, 2), ("weight", 3, True, 1),
+    ("weight", 0, False, 1), ("forward", 3), ("weight", 1, True, 2), ("weight", 1, False, 1), ("weight", 2, True, 2),
+    ("weight", 3, True, 2), ("forward", 1), ("weight", 0, False, 2), ("weight", 1, False, 2), ("forward", 2),
+    ("weight", 2, True, 3), ("weight", 3, True, 3), ("weight", 2, False, 2), ("weight", 2, False, 1),
+    ("weight", 1, True, 3), ("weight", 1, False, 3), ("weight", 2, True, 4), ("weight", 0, False, 3),
+    ("weight", 3, False, 0), ("weight", 0, True, 3), ("weight", 3, False, 1), ("weight", 3, False, 2),
+    ("weight", 3, True, 4), ("weight", 3, False, 3), ("enter",), ("weight", 1, True, 4), ("weight", 1, False, 4),
+    ("weight", 0, True, 4), ("weight", 2, False, 4), ("weight", 0, False, 4), ("weight", 2, False, 3),
+    ("weight", 3, False, 4),
+)
 
 
 def norm_rows(values):
@@ -57,6 +84,11 @@
         natural = ((part & (ROWS - 1)) >> EACH_BITS << 3) + (part >> ROWS_BITS << EACH_BITS) + (part & (EACH - 1))
         return jnp.where(natural == own, 1.0, 0.0).astype(BF)
 
+    barrier = pltpu.get_barrier_semaphore()
+    peers = [(f_z, t), (f_core, t), (at_y(f, 1), t), (at_y(f, -1), t)]
+    peers += [(f, tensor_at(dx, 0)) for dx in (1, 2, 3)] + [(f, tensor_at(0, dz)) for dz in (1, 2, 3)]
+    for peer in peers:
+        pl.semaphore_signal(barrier, inc=1, device_id=peer, device_id_type=MESH)
     pltpu.make_async_copy(x_in, x_own, local_sem.at[0]).start()
     pltpu.make_async_copy(gain1_in, gain1, local_sem.at[1]).start()
     pltpu.make_async_copy(gain2_in, gain2, local_sem.at[2]).start()
@@ -67,11 +99,6 @@
     def placed(ref, k):
         pltpu.make_async_copy(ref, ref, local_sem.at[k]).wait()
 
-    barrier = pltpu.get_barrier_semaphore()
-    peers = [(f_z, t), (f_core, t), (at_y(f, 1), t), (at_y(f, -1), t)]
-    peers += [(f, tensor_at(dx, 0)) for dx in (1, 2, 3)] + [(f, tensor_at(0, dz)) for dz in (1, 2, 3)]
-    for peer in peers:
-        pl.semaphore_signal(barrier, inc=1, device_id=peer, device_id_type=MESH)
     placed(x_own, 0)
     placed(w.at[0, f], 3)
     xs[t] = jnp.dot(part_order(0), x_own[...], preferred_element_type=F32).astype(BF)
@@ -98,7 +125,7 @@
 
     def w_rank(b, i, own, k):
         base = f if own else f_z
-        early = i < PIECES[b] // 2
+        early = b == 1 or i < PIECES[b] // 2
         kind = k - 1 if own else 4 + k
         rows = 64 // PIECES[b]
         both = k in (1, 2, 3)
@@ -170,19 +197,13 @@
 
     order = (2, 1, 3, 0)
 
-    groups = []
-
     def project(b, k, dz, both):
-        n = len(groups)
-        if n >= 2:
-            left(from_x.at[0, 0, 0], rx_send.at[n % 2])
         for dx in (2, 1, 3, 0):
             slot = 2 * tensor_at(dx, dz)
             weight = w[b, pl.ds(slot, 2), :, 640:1024].reshape(128, 384)
             terms[b, k, dx, dz] = lax.dot_general(both, weight, NT, preferred_element_type=F32).astype(BF)
             if dx:
-                send(terms.at[b, k, dx, dz], from_x.at[b, k, dz, dx - 1], rx_send.at[n % 2], rx_recv.at[b, k, dz], (f, tensor_at(dx, 0)))
-        groups.append(n)
+                send(terms.at[b, k, dx, dz], from_x.at[b, k, dz, dx - 1], rx_send.at[0], rx_recv.at[b, k, dz], (f, tensor_at(dx, 0)))
 
     def sum_x(b, k, dz):
         arrived(from_x.at[b, k, dz], rx_recv.at[b, k, dz])
@@ -216,112 +237,62 @@
         arrived(turned.at[k, pl.ds(0, 31)], turn_recv.at[k])
         xt[k, t] = turned[k].reshape(ROWS, 128).astype(BF)
 
-    quarters = range(PIECES[0])
-    for i in quarters[:1]:
+    w_first(0, 0)
+    gather_own(xs, 0)
+    for i in range(1, PIECES[0]):
         w_first(0, i)
-    gather_own(xs, 0)
-    for i in quarters[1:]:
-        w_first(0, i)
-    for i in quarters:
-        w_rank(0, i, True, 1)
-    for i in quarters:
-        w_rank(0, i, False, 0)
-    for i in (0, 1):
-        w_rank(0, i, True, 2)
-    gather_forward(xs, 0, 3 - 2 * lo)
-    for i in (2, 3):
-        w_rank(0, i, True, 2)
-    for i in quarters:
-        w_rank(0, i, False, 1)
-    for i in (0, 1):
-        w_rank(0, i, True, 3)
-    gather_forward(xs, 0, 1 + 2 * lo)
-    w_rank(0, 2, True, 3)
-    gather_forward(xs, 0, 2)
-    w_rank(0, 2, False, 2)
-    w_rank(0, 3, True, 3)
-    w_rank(0, 3, False, 2)
-    for i in (0, 1):
-        w_rank(0, i, False, 2)
-    for i in quarters:
-        w_rank(0, i, True, 4)
-    for i in (2, 3, 0, 1):
-        w_rank(0, i, False, 3)
-    w_rank(0, 2, False, 4)
-    gather_rest(xs, 0)
-    placed(gain1, 1)
-    normalize(xs, 256, gain1)
-    for i in (3, 0, 1):
-        w_rank(0, i, False, 4)
-
-    def second(k):
-        for i in range(PIECES[1]):
-            if 0 < k < 5:
-                w_rank(1, i, True, k)
-            if k > 0:
-                w_rank(1, i, False, k - 1)
-            else:
-                w_first(1, i)
-
-    blocks = [(k, dz) for k in range(PARTS) for dz in order]
-
-    def branch(b, rows_of, after_sum):
-        issued = 0
-        for i, (k, dz) in enumerate(blocks):
-            for ahead in blocks[issued : i + 4]:
-                project(b, *ahead, rows_of(*ahead))
-                issued += 1
-            sum_x(b, k, dz)
-            after_sum(k, dz)
+    for step, *at in PLAN_FIRST:
+        if step == "weight":
+            w_rank(0, *at)
+        elif step == "forward":
+            gather_forward(xs, 0, {1: 1 + 2 * lo, 2: 2, 3: 3 - 2 * lo}[at[0]])
+        elif step == "enter":
+            gather_rest(xs, 0)
+            placed(gain1, 1)
+            normalize(xs, 256, gain1)
 
     w_core(0)
-    both = inner(0, 256)
+    branches = {}
+    entered = inner(0, 256)
+    for k in range(PARTS):
+        branches[0, k] = entered[k * ROWS : (k + 1) * ROWS]
     placed(w.at[1, f], 4)
     placed(gain2, 2)
-    second(0)
-
-    def turn_last(k, dz):
-        if k and dz == order[1]:
-            turn(k - 1)
-
-    branch(0, lambda k, dz: both[k * ROWS : (k + 1) * ROWS], turn_last)
-    second(1)
-    turn(PARTS - 1)
-    for k in range(PARTS):
-        turn_done(k)
-        gather_own(xt.at[k], k + 1)
-        if k == 0:
-            second(2)
-    for k in range(PARTS):
-        for dz in (1, 3, 2):
-            gather_forward(xt.at[k], k + 1, dz)
-        if k == 0:
-            second(3)
-            second(4)
-
-    rows2 = {}
-
-    def enter(k, dz):
-        if k not in rows2:
+
+    for step, *at in PLAN:
+        if step == "first":
+            for i in range(PIECES[1]):
+                w_first(1, i)
+        elif step == "weight":
+            w_rank(1, *at)
+        elif step == "project":
+            project(*at, branches[at[0], at[1]])
+        elif step == "sum":
+            sum_x(*at)
+        elif step == "turn":
+            turn(*at)
+        elif step == "turned":
+            turn_done(*at)
+            gather_own(xt.at[at[0]], at[0] + 1)
+        elif step == "forward":
+            gather_forward(xt.at[at[0]], at[0] + 1, at[1])
+        elif step == "enter":
+            k = at[0]
             gather_rest(xt.at[k], k + 1)
             normalize(xt.at[k], ROWS, gain2)
             if k == 0:
-                second(5)
                 w_core(1)
-            rows2[k] = inner(1, ROWS)
-        return rows2[k]
-
-    branch(1, enter, lambda k, dz: None)
+            branches[1, k] = inner(1, ROWS)
     total = jnp.concatenate([sum_z(1, k) for k in range(PARTS)], axis=0)
     kept = jnp.concatenate([turned[k].reshape(ROWS, 128) for k in range(PARTS)], axis=0)
     y_out[...] = jnp.dot(part_order(1), (kept + total).astype(BF), preferred_element_type=F32).astype(BF)
     for b in range(2):
         left(w.at[b, pl.ds(0, used[b] // PIECES[b])], w_send.at[b])
-        left(from_x.at[0, 0, 0], rx_send.at[b])
     left(xs.at[pl.ds(0, 15)], ag_send.at[0])
     for k in range(PARTS):
         left(xt.at[k, pl.ds(0, 15)], ag_send.at[k + 1])
         left(mid.at[k, pl.ds(0, 31)], turn_send.at[k])
+    left(from_x, rx_send.at[0])
     left(to_z, rz_send.at[0])
 
 

time: 96.1 us -> 92.6 us (0.964)
  Pallas kernels: 94.4 us -> 90.9 us
    pallas_call x1, Pallas kernels: 94.4 us -> 90.9 us  [body(): pl.pallas_call(kernel, out_shape=jax.ShapeDtypeStruct((256, 128), BF), in...]
where the time goes in v3:
time: 92.6 us; the launch traced here: 92.4 us
  Pallas kernels  90.9 us (98%)
  local copies, waits for them, and re-layouts  1.47 us (2%)
    pallas_call x1, Pallas kernels, body(): pl.pallas_call(kernel, out_shape=jax.ShapeDtypeStruct((256, 128), BF), in...  90.9 us

profile of v3, /device:TPU:1, one launch (start us, length us, event | category | flops | bytes accessed | tf_op | source)
XLA Modules:
  0.0 92.4 jit_solution(2956395636518451261)
XLA Ops:
  0.0 90.9 %shard_map.109 = bf16[256,128]{1,0:T(8,128)(2,1)} custom-call(bf16[256,128]{1,0:T(8,128)(2,1)} %bitcast.7, f32[16,1,128]{2,1,0:T(1,128)} %bitcast.10, f32[16,1,128]{2,1,0:T(1,128)} %bitcast.11, bf16[3,64,128]{2,1,0:T(8,128)(2,1)} %bitcast.8, bf16[64,128]{1,0:T(8,128)(2,1)} %out1.1, bf16[64,256]{1,0:T(8,128)(2,1)} %up1.1, bf16[64,256]{1,0:T(8,128)(2,1)} %down1.1, ...), custom_call_target="tpu_custom_call" | custom-call | tf_op jit(solution)/shard_map/pallas_call | solution.py:313
  90.9 1.5 %copy.13 = bf16[32,8,128]{2,1,0:T(8,128)(2,1)} copy(bf16[32,8,128]{2,1,0:T(8,128)(2,1)} %bitcast.6) | data formatting | bytes 131072

commit v4 on v3

--- a/solution.py
+++ b/solution.py
@@ -29,18 +29,6 @@
     ("project", 1, 0, 1), ("project", 1, 0, 3), ("enter", 1), ("project", 1, 1, 2), ("project", 1, 1, 1), ("sum", 1, 0, 2),
     ("project", 1, 1, 3), ("sum", 1, 0, 1), ("sum", 1, 0, 3), ("sum", 1, 1, 2), ("project", 1, 0, 0), ("project", 1, 1, 0),
     ("sum", 1, 1, 1), ("sum", 1, 1, 3), ("sum", 1, 0, 0), ("sum", 1, 1, 0),
-)
-PLAN_FIRST = (
-    ("weight", 0, True, 1), ("weight", 1, True, 1), ("weight", 0, False, 0), ("weight", 1, False, 0),
-    ("weight", 2, False, 0), ("weight", 2, True, 1), ("weight", 0, True, 2), ("weight", 3, True, 1),
-    ("weight", 0, False, 1), ("forward", 3), ("weight", 1, True, 2), ("weight", 1, False, 1), ("weight", 2, True, 2),
-    ("weight", 3, True, 2), ("forward", 1), ("weight", 0, False, 2), ("weight", 1, False, 2), ("forward", 2),
-    ("weight", 2, True, 3), ("weight", 3, True, 3), ("weight", 2, False, 2), ("weight", 2, False, 1),
-    ("weight", 1, True, 3), ("weight", 1, False, 3), ("weight", 2, True, 4), ("weight", 0, False, 3),
-    ("weight", 3, False, 0), ("weight", 0, True, 3), ("weight", 3, False, 1), ("weight", 3, False, 2),
-    ("weight", 3, True, 4), ("weight", 3, False, 3), ("enter",), ("weight", 1, True, 4), ("weight", 1, False, 4),
-    ("weight", 0, True, 4), ("weight", 2, False, 4), ("weight", 0, False, 4), ("weight", 2, False, 3),
-    ("weight", 3, False, 4),
 )
 
 
@@ -153,7 +141,7 @@
         send(slot, slot, ag_send.at[k], ag_recv.at[k, to_dz], (f, tensor_at(to_dx, to_dz)))
 
     def gather_own(view, k):
-        for dz in (2, 1, 3):
+        for dz in (1, 3, 2):
             gather_push(view, k, 0, 0, 0, dz)
         for dx in (2, 1, 3):
             gather_push(view, k, 0, 0, dx, 0)
@@ -237,19 +225,41 @@
         arrived(turned.at[k, pl.ds(0, 31)], turn_recv.at[k])
         xt[k, t] = turned[k].reshape(ROWS, 128).astype(BF)
 
-    w_first(0, 0)
+    pieces = range(PIECES[0])
+    early, late = pieces[: PIECES[0] // 2], pieces[PIECES[0] // 2 :]
+    for i in pieces:
+        w_first(0, i)
     gather_own(xs, 0)
-    for i in range(1, PIECES[0]):
-        w_first(0, i)
-    for step, *at in PLAN_FIRST:
-        if step == "weight":
-            w_rank(0, *at)
-        elif step == "forward":
-            gather_forward(xs, 0, {1: 1 + 2 * lo, 2: 2, 3: 3 - 2 * lo}[at[0]])
-        elif step == "enter":
-            gather_rest(xs, 0)
-            placed(gain1, 1)
-            normalize(xs, 256, gain1)
+    for i in pieces:
+        w_rank(0, i, True, 1)
+    for i in pieces:
+        w_rank(0, i, False, 0)
+    for i in early:
+        w_rank(0, i, True, 2)
+    gather_forward(xs, 0, 3 - 2 * lo)
+    for i in late:
+        w_rank(0, i, True, 2)
+    for i in pieces:
+        w_rank(0, i, False, 1)
+    for i in early:
+        w_rank(0, i, True, 3)
+    gather_forward(xs, 0, 1 + 2 * lo)
+    for i in late:
+        w_rank(0, i, True, 3)
+    gather_forward(xs, 0, 2)
+    for i in (*late, *early):
+        w_rank(0, i, False, 2)
+    for i in pieces:
+        w_rank(0, i, True, 4)
+    for i in (*late, *early):
+        w_rank(0, i, False, 3)
+    for i in late:
+        w_rank(0, i, False, 4)
+    gather_rest(xs, 0)
+    placed(gain1, 1)
+    normalize(xs, 256, gain1)
+    for i in early:
+        w_rank(0, i, False, 4)
 
     w_core(0)
     branches = {}

time: 92.6 us -> 90.8 us (0.981)
  Pallas kernels: 90.9 us -> 89.1 us
    pallas_call x1, Pallas kernels: 90.9 us -> 89.1 us  [body(): pl.pallas_call(kernel, out_shape=jax.ShapeDtypeStruct((256, 128), BF), in...]
where the time goes in v4:
time: 90.8 us; the launch traced here: 90.6 us
  Pallas kernels  89.1 us (98%)
  local copies, waits for them, and re-layouts  1.47 us (2%)
    pallas_call x1, Pallas kernels, body(): pl.pallas_call(kernel, out_shape=jax.ShapeDtypeStruct((256, 128), BF), in...  89.1 us

profile of v4, /device:TPU:1, one launch (start us, length us, event | category | flops | bytes accessed | tf_op | source)
XLA Modules:
  0.0 90.6 jit_solution(5989850143951537436)
XLA Ops:
  0.0 89.1 %shard_map.109 = bf16[256,128]{1,0:T(8,128)(2,1)} custom-call(bf16[256,128]{1,0:T(8,128)(2,1)} %bitcast.7, f32[16,1,128]{2,1,0:T(1,128)} %bitcast.10, f32[16,1,128]{2,1,0:T(1,128)} %bitcast.11, bf16[3,64,128]{2,1,0:T(8,128)(2,1)} %bitcast.8, bf16[64,128]{1,0:T(8,128)(2,1)} %out1.1, bf16[64,256]{1,0:T(8,128)(2,1)} %up1.1, bf16[64,256]{1,0:T(8,128)(2,1)} %down1.1, ...), custom_call_target="tpu_custom_call" | custom-call | tf_op jit(solution)/shard_map/pallas_call | solution.py:323
  89.1 1.5 %copy.13 = bf16[32,8,128]{2,1,0:T(8,128)(2,1)} copy(bf16[32,8,128]{2,1,0:T(8,128)(2,1)} %bitcast.6) | data formatting | bytes 131072

commit v5 on v4

--- a/solution.py
+++ b/solution.py
@@ -17,7 +17,7 @@
 PIECES = (4, 2)
 
 PLAN = (
-    ("project", 0, 0, 2), ("first",), ("project", 0, 0, 1), ("project", 0, 0, 3), ("project", 0, 0, 0),
+    ("first",), ("project", 0, 0, 2), ("project", 0, 0, 1), ("project", 0, 0, 3), ("project", 0, 0, 0),
     ("weight", 0, False, 0), ("project", 0, 1, 2), ("sum", 0, 0, 2), ("project", 0, 1, 1), ("weight", 1, True, 1),
     ("sum", 0, 0, 1), ("project", 0, 1, 3), ("sum", 0, 0, 3), ("weight", 0, False, 1), ("project", 0, 1, 0),
     ("weight", 1, False, 0), ("sum", 0, 1, 2), ("sum", 0, 0, 0), ("sum", 0, 1, 1), ("sum", 0, 1, 3), ("turn", 0),
@@ -186,12 +186,13 @@
     order = (2, 1, 3, 0)
 
     def project(b, k, dz, both):
-        for dx in (2, 1, 3, 0):
-            slot = 2 * tensor_at(dx, dz)
-            weight = w[b, pl.ds(slot, 2), :, 640:1024].reshape(128, 384)
-            terms[b, k, dx, dz] = lax.dot_general(both, weight, NT, preferred_element_type=F32).astype(BF)
-            if dx:
-                send(terms.at[b, k, dx, dz], from_x.at[b, k, dz, dx - 1], rx_send.at[0], rx_recv.at[b, k, dz], (f, tensor_at(dx, 0)))
+        for pair in ((2, 1), (3, 0)):
+            weight = [w[b, pl.ds(2 * tensor_at(dx, dz), 2), :, 640:1024].reshape(128, 384) for dx in pair]
+            product = lax.dot_general(both, jnp.concatenate(weight, axis=0), NT, preferred_element_type=F32).astype(BF)
+            for n, dx in enumerate(pair):
+                terms[b, k, dx, dz] = product[:, 128 * n : 128 * (n + 1)]
+                if dx:
+                    send(terms.at[b, k, dx, dz], from_x.at[b, k, dz, dx - 1], rx_send.at[0], rx_recv.at[b, k, dz], (f, tensor_at(dx, 0)))
 
     def sum_x(b, k, dz):
         arrived(from_x.at[b, k, dz], rx_recv.at[b, k, dz])

time: 90.8 us -> 90.8 us (level)
  no operation moved by 1% of the time
where the time goes in v5:
time: 90.8 us; the launch traced here: 90.6 us
  Pallas kernels  89.1 us (98%)
  local copies, waits for them, and re-layouts  1.47 us (2%)
    pallas_call x1, Pallas kernels, body(): pl.pallas_call(kernel, out_shape=jax.ShapeDtypeStruct((256, 128), BF), in...  89.1 us

profile of v5, /device:TPU:1, one launch (start us, length us, event | category | flops | bytes accessed | tf_op | source)
XLA Modules:
  0.0 90.6 jit_solution(2785573145876783821)
XLA Ops:
  0.0 89.1 %shard_map.109 = bf16[256,128]{1,0:T(8,128)(2,1)} custom-call(bf16[256,128]{1,0:T(8,128)(2,1)} %bitcast.7, f32[16,1,128]{2,1,0:T(1,128)} %bitcast.10, f32[16,1,128]{2,1,0:T(1,128)} %bitcast.11, bf16[3,64,128]{2,1,0:T(8,128)(2,1)} %bitcast.8, bf16[64,128]{1,0:T(8,128)(2,1)} %out1.1, bf16[64,256]{1,0:T(8,128)(2,1)} %up1.1, bf16[64,256]{1,0:T(8,128)(2,1)} %down1.1, ...), custom_call_target="tpu_custom_call" | custom-call | tf_op jit(solution)/shard_map/pallas_call | solution.py:324
  89.1 1.5 %copy.13 = bf16[32,8,128]{2,1,0:T(8,128)(2,1)} copy(bf16[32,8,128]{2,1,0:T(8,128)(2,1)} %bitcast.6) | data formatting | bytes 131072

commit v6 on v4

--- a/solution.py
+++ b/solution.py
@@ -17,7 +17,7 @@
 PIECES = (4, 2)
 
 PLAN = (
-    ("project", 0, 0, 2), ("first",), ("project", 0, 0, 1), ("project", 0, 0, 3), ("project", 0, 0, 0),
+    ("first",), ("project", 0, 0, 2), ("project", 0, 0, 1), ("project", 0, 0, 3), ("project", 0, 0, 0),
     ("weight", 0, False, 0), ("project", 0, 1, 2), ("sum", 0, 0, 2), ("project", 0, 1, 1), ("weight", 1, True, 1),
     ("sum", 0, 0, 1), ("project", 0, 1, 3), ("sum", 0, 0, 3), ("weight", 0, False, 1), ("project", 0, 1, 0),
     ("weight", 1, False, 0), ("sum", 0, 1, 2), ("sum", 0, 0, 0), ("sum", 0, 1, 1), ("sum", 0, 1, 3), ("turn", 0),

time: 90.8 us -> 90.9 us (level)
  no operation moved by 1% of the time
where the time goes in v6:
time: 90.9 us; the launch traced here: 90.7 us
  Pallas kernels  89.2 us (98%)
  local copies, waits for them, and re-layouts  1.47 us (2%)
    pallas_call x1, Pallas kernels, body(): pl.pallas_call(kernel, out_shape=jax.ShapeDtypeStruct((256, 128), BF), in...  89.2 us

profile of v6, /device:TPU:1, one launch (start us, length us, event | category | flops | bytes accessed | tf_op | source)
XLA Modules:
  0.0 90.7 jit_solution(12708819786153268698)
XLA Ops:
  0.0 89.2 %shard_map.109 = bf16[256,128]{1,0:T(8,128)(2,1)} custom-call(bf16[256,128]{1,0:T(8,128)(2,1)} %bitcast.7, f32[16,1,128]{2,1,0:T(1,128)} %bitcast.10, f32[16,1,128]{2,1,0:T(1,128)} %bitcast.11, bf16[3,64,128]{2,1,0:T(8,128)(2,1)} %bitcast.8, bf16[64,128]{1,0:T(8,128)(2,1)} %out1.1, bf16[64,256]{1,0:T(8,128)(2,1)} %up1.1, bf16[64,256]{1,0:T(8,128)(2,1)} %down1.1, ...), custom_call_target="tpu_custom_call" | custom-call | tf_op jit(solution)/shard_map/pallas_call | solution.py:323
  89.2 1.5 %copy.13 = bf16[32,8,128]{2,1,0:T(8,128)(2,1)} copy(bf16[32,8,128]{2,1,0:T(8,128)(2,1)} %bitcast.6) | data formatting | bytes 131072
